TPU v7x, 512 devices: a whole 4x4x16 slice. The times are simulated.
512 devices in a mesh: seq: 32 (over x, y, core), key: 16 (over z).
Axes of the slice: x: 4, y: 4, z: 16, core: 2. Of those that a mesh axis runs over, the one named last changes fastest.
Arguments:
- query_rows: bfloat16 [8192, 16, 256], P('seq', None, 'key'), may hold values from -0.375 to 0.375
- key_rows: bfloat16 [8192, 16, 256], P('seq', None, 'key'), may hold values from -0.1875 to 0.1875
- value_rows: bfloat16 [8192, 16, 256], P('seq', 'key'), may hold values from -6 to 6
- out_grad: bfloat16 [8192, 16, 256], P('seq', 'key')
- log_gates: float32 [16, 8192], P('key', 'seq'), may hold values from -0.8 to 0, as said below
- write_rate: float32 [16, 8192], P('key', 'seq'), may hold values from 0.1 to 0.8
- group_inverse: bfloat16 [64, 16, 128, 128], P('seq', 'key'), as said below
- states: bfloat16 [64, 16, 256, 256], P('seq', None, 'key'), may hold values from -0.75 to 0.75
Outputs:
- grad_query: bfloat16 [8192, 16, 256], P('seq', None, 'key')
- grad_key: bfloat16 [8192, 16, 256], P('seq', None, 'key')
- grad_value: bfloat16 [8192, 16, 256], P('seq', 'key')
- grad_square: float32 [], replicated
Inputs may be any that keep to these rules, and one draw needn't show every extreme that they name: `group_inverse`: each group's matrix is unit lower triangular: ones on the diagonal, zeros above it. `log_gates`: every entry is the logarithm of a decay factor, never positive.
All inputs are finite; a program needn't handle non-finite values.
Results may differ from a plain program's by a relative error of at most 0.007.
Values may be sent and summed in bfloat16 or wider, within the bound.
No kernel may reach another device: no remote copies, remote signals or barrier semaphores. Data moves between devices by JAX's collectives and lax.ppermute only.
A program may use at most 128 MiB of HBM per device.

v0:
```python
import jax
import jax.numpy as jnp
from jax import lax
from jax.sharding import PartitionSpec as P

highest_mode = lax.Precision.HIGHEST


def from_behind(value, axis, steps):
    count = lax.axis_size(axis)
    first, last = (max(0, -steps), min(count, count - steps))
    return lax.ppermute(value, axis, [(source, source + steps) for source in range(first, last)])


def mixed_dot(form, left, right):
    return jnp.einsum(form, left, right, preferred_element_type=jnp.float32)


def precise_product(form, left, right):
    return jnp.einsum(form, left.astype(jnp.float32), right, precision=highest_mode)


def linear_part(state_in, write_block, key_block, decay_block):
    through = precise_product("thk,hkm->thm", key_block, state_in)
    return decay_block[:, None, None] * state_in - precise_product(
        "thk,thm->hkm", write_block, through
    )


def device_map(state_out, written_keys, key_result, end_decay, offset_term):

    def group_step(state_in, pieces):
        write_block, key_block, decay_block, offset_block = pieces
        return (linear_part(state_in, write_block, key_block, decay_block) + offset_block, state_in)

    return lax.scan(
        group_step, state_out, (written_keys, key_result, end_decay, offset_term), reverse=True
    )


def token_wise(factor):
    return jnp.transpose(factor, (0, 2, 1))[:, :, :, None]


def square_sum(array):
    return jnp.sum(jnp.square(array.astype(jnp.float32)))


def local(query_rows, key_rows, value_rows, out_grad, log_gates, write_rate, group_inverse, states):
    halfway_point = jnp.bfloat16
    query_heads, key_heads, state_heads = (
        lax.all_to_all(query_rows, "key", split_axis=1, concat_axis=2, tiled=True),
        lax.all_to_all(key_rows, "key", split_axis=1, concat_axis=2, tiled=True),
        lax.all_to_all(states, "key", split_axis=1, concat_axis=2, tiled=True),
    )
    group_count, head_local, group_len, _ = group_inverse.shape
    token_count, _, key_width = query_heads.shape
    value_width = value_rows.shape[2]
    query_blk = query_heads.reshape(group_count, group_len, head_local, key_width)
    key_blk = key_heads.reshape(group_count, group_len, head_local, key_width)
    value_blk = value_rows.reshape(group_count, group_len, head_local, value_width)
    grad_blk = out_grad.reshape(group_count, group_len, head_local, value_width)
    gate_blk = jnp.transpose(log_gates.reshape(head_local, group_count, group_len), (1, 0, 2))
    rate_blk = jnp.transpose(write_rate.reshape(head_local, group_count, group_len), (1, 0, 2))
    gamma = jnp.cumsum(gate_blk, axis=2)
    final_gamma_value = gamma[:, :, -1:]
    incoming_decay = jnp.exp(gamma)
    outgoing_decay = jnp.exp(final_gamma_value - gamma)
    row_ids = lax.broadcasted_iota(jnp.int32, (group_len, group_len), 0)
    col_ids = lax.broadcasted_iota(jnp.int32, (group_len, group_len), 1)
    lower = row_ids >= col_ids
    spread = gamma[:, :, :, None] - gamma[:, :, None, :]
    decay_mask = jnp.where(lower, jnp.exp(jnp.where(lower, spread, 0.0)), 0.0)
    key_scaled = (key_blk * token_wise(rate_blk * incoming_decay)).astype(halfway_point)
    written_keys = mixed_dot("nhts,nshk->nthk", group_inverse, key_scaled).astype(halfway_point)
    scaled_values = (value_blk * token_wise(rate_blk)).astype(halfway_point)
    fresh_values = (
        mixed_dot("nhts,nshv->nthv", group_inverse, scaled_values)
        - mixed_dot("nthk,nhkv->nthv", written_keys, state_heads)
    ).astype(halfway_point)
    score_mat = (mixed_dot("nthk,nshk->nhts", query_blk, key_blk) * decay_mask).astype(
        halfway_point
    )
    key_result = (key_blk * token_wise(outgoing_decay)).astype(halfway_point)
    incoming_query = (query_blk * token_wise(incoming_decay)).astype(halfway_point)
    inner_gradient = mixed_dot("nhts,nthv->nshv", score_mat, grad_blk)
    offset_term = mixed_dot("nthk,nthv->nhkv", incoming_query, grad_blk) - precise_product(
        "nthk,nthv->nhkv", written_keys, inner_gradient
    )
    end_decay = jnp.exp(final_gamma_value[:, :, 0])
    empty_state = jnp.zeros((head_local, key_width, value_width), jnp.float32)

    def relay_hop(hop_index, incoming):
        state_in, _ = device_map(incoming, written_keys, key_result, end_decay, offset_term)
        return from_behind(state_in, "seq", -1)

    state_out = lax.fori_loop(0, lax.axis_size("seq") - 1, relay_hop, empty_state)
    _, state_gradient = device_map(state_out, written_keys, key_result, end_decay, offset_term)
    value_rounding = (
        inner_gradient + precise_product("nthk,nhkv->nthv", key_result, state_gradient)
    ).astype(halfway_point)
    value_grad_blk = (
        token_wise(rate_blk) * mixed_dot("nhts,nthv->nshv", group_inverse, value_rounding)
    ).astype(halfway_point)
    score_gradient = (mixed_dot("nthv,nshv->nhts", grad_blk, fresh_values) * decay_mask).astype(
        halfway_point
    )
    write_gradient = (-mixed_dot("nthv,nhkv->nthk", value_rounding, state_heads)).astype(
        halfway_point
    )
    state_rounding = state_gradient.astype(halfway_point)
    query_grad_blk = (
        token_wise(incoming_decay) * mixed_dot("nthv,nhkv->nthk", grad_blk, state_heads)
        + mixed_dot("nhts,nshk->nthk", score_gradient, key_blk)
    ).astype(halfway_point)
    key_grad_blk = (
        mixed_dot("nhts,nthk->nshk", score_gradient, query_blk)
        + token_wise(outgoing_decay) * mixed_dot("nthv,nhkv->nthk", fresh_values, state_rounding)
        + token_wise(rate_blk * incoming_decay)
        * mixed_dot("nhts,nthk->nshk", group_inverse, write_gradient)
    ).astype(halfway_point)
    query_grad_heads = query_grad_blk.reshape(token_count, head_local, key_width)
    key_grad_heads = key_grad_blk.reshape(token_count, head_local, key_width)
    grad_value = value_grad_blk.reshape(token_count, head_local, value_width)
    grad_query, grad_key = (
        lax.all_to_all(query_grad_heads, "key", split_axis=2, concat_axis=1, tiled=True),
        lax.all_to_all(key_grad_heads, "key", split_axis=2, concat_axis=1, tiled=True),
    )
    value_square = square_sum(grad_value)
    partial_value = square_sum(grad_query) + square_sum(grad_key) + value_square
    summed = lax.psum(partial_value, ("seq", "key"))
    entries = (
        token_count * lax.axis_size("seq") * query_rows.shape[1] * (2 * key_width + value_width)
    )
    return (grad_query, grad_key, grad_value, summed / entries)


def solution(mesh):
    in_specs = (
        P("seq", None, "key"),
        P("seq", None, "key"),
        P("seq", "key", None),
        P("seq", "key", None),
        P("key", "seq"),
        P("key", "seq"),
        P("seq", "key", None, None),
        P("seq", None, "key", None),
    )
    out_specs = (P("seq", None, "key"), P("seq", None, "key"), P("seq", "key", None), P())
    return jax.shard_map(local, mesh=mesh, in_specs=in_specs, out_specs=out_specs, check_vma=False)
```

profile of v0, /device:TPU:1, one launch (start us, length us, event | category | flops | bytes accessed | tf_op | source)
XLA Modules:
  0.0 631.2 jit_solution(10819537718962490288)
XLA Ops:
  0.7 15.9 %all-to-all-start.1 = ((bf16[256,16,16]{0,2,1:T(8,128)(2,1)}), bf16[256,16,16]{0,2,1:T(8,128)(2,1)S(1)}, u32[]{:S(2)}, u32[]{:S(2)}) async-start(bf16[256,16,16]{0,2,1:T(8,128)(2,1)} %param.15), calls=%async_computation.1 | async-start | bytes 262144 | tf_op jit(solution)/shard_map/all_to_all | solution.py:53
  17.9 10.7 %all-to-all-done.1 = bf16[256,16,16]{0,2,1:T(8,128)(2,1)S(1)} async-done(((bf16[256,16,16]{0,2,1:T(8,128)(2,1)}), bf16[256,16,16]{0,2,1:T(8,128)(2,1)S(1)}, u32[]{:S(2)}, u32[]{:S(2)}) %all-to-all-start.1) | async-done | bytes 131104 | tf_op jit(solution)/shard_map/all_to_all | solution.py:53
  28.6 5.9 all-to-all-start.3
  36.8 9.7 %all-to-all-done.3 = bf16[256,16,16]{0,2,1:T(8,128)(2,1)S(1)} async-done(((bf16[256,16,16]{0,2,1:T(8,128)(2,1)}), bf16[256,16,16]{0,2,1:T(8,128)(2,1)S(1)}, u32[]{:S(2)}, u32[]{:S(2)}) %all-to-all-start.3) | async-done | bytes 131104 | tf_op jit(solution)/shard_map/all_to_all | solution.py:52
  54.0 393.7 %while.57 = (s32[]{:T(128)}, f32[1,256,256]{2,1,0:T(8,128)S(1)}, f32[2,1]{0,1:T(1,128)S(1)}, bf16[2,128,1,256]{3,1,2,0:T(8,128)(2,1)S(1)}, bf16[2,128,1,256]{3,1...) while((s32[]{:T(128)}, f32[1,256,256]{2,1,0:T(8,128)S(1)}, ...), condition=%wide.region_4.5_spmd, body=%wide.region_1.4_spmd.sunk | while | flops 201523200 | bytes 3015986 | solution.py:97
  72.9 5.8 collective-permute-done
  107.3 5.8 collective-permute-done
  118.7 5.8 collective-permute-done
  141.7 5.8 collective-permute-done
  153.1 5.8 collective-permute-done
  210.5 6.5 %collective-permute-done = f32[1,256,256]{2,1,0:T(8,128)S(1)} collective-permute-done((f32[1,256,256]{2,1,0:T(8,128)S(1)}, f32[1,256,256]{2,1,0:T(8,128)S(1)}, u32[]{:S(2)}, u32[]{:S(2)}) %collective-permute-start) | collective-permute-done | bytes 262176 | tf_op jit(solution)/shard_map/while/body/eval_jaxpr/ppermute | solution.py:12
  222.6 7.9 %collective-permute-done = f32[1,256,256]{2,1,0:T(8,128)S(1)} collective-permute-done((f32[1,256,256]{2,1,0:T(8,128)S(1)}, f32[1,256,256]{2,1,0:T(8,128)S(1)}, u32[]{:S(2)}, u32[]{:S(2)}) %collective-permute-start) | collective-permute-done | bytes 262176 | tf_op jit(solution)/shard_map/while/body/eval_jaxpr/ppermute | solution.py:12
  236.2 7.9 %collective-permute-done = f32[1,256,256]{2,1,0:T(8,128)S(1)} collective-permute-done((f32[1,256,256]{2,1,0:T(8,128)S(1)}, f32[1,256,256]{2,1,0:T(8,128)S(1)}, u32[]{:S(2)}, u32[]{:S(2)}) %collective-permute-start) | collective-permute-done | bytes 262176 | tf_op jit(solution)/shard_map/while/body/eval_jaxpr/ppermute | solution.py:12
  249.8 7.9 %collective-permute-done = f32[1,256,256]{2,1,0:T(8,128)S(1)} collective-permute-done((f32[1,256,256]{2,1,0:T(8,128)S(1)}, f32[1,256,256]{2,1,0:T(8,128)S(1)}, u32[]{:S(2)}, u32[]{:S(2)}) %collective-permute-start) | collective-permute-done | bytes 262176 | tf_op jit(solution)/shard_map/while/body/eval_jaxpr/ppermute | solution.py:12
  263.4 7.9 %collective-permute-done = f32[1,256,256]{2,1,0:T(8,128)S(1)} collective-permute-done((f32[1,256,256]{2,1,0:T(8,128)S(1)}, f32[1,256,256]{2,1,0:T(8,128)S(1)}, u32[]{:S(2)}, u32[]{:S(2)}) %collective-permute-start) | collective-permute-done | bytes 262176 | tf_op jit(solution)/shard_map/while/body/eval_jaxpr/ppermute | solution.py:12
  276.9 7.9 %collective-permute-done = f32[1,256,256]{2,1,0:T(8,128)S(1)} collective-permute-done((f32[1,256,256]{2,1,0:T(8,128)S(1)}, f32[1,256,256]{2,1,0:T(8,128)S(1)}, u32[]{:S(2)}, u32[]{:S(2)}) %collective-permute-start) | collective-permute-done | bytes 262176 | tf_op jit(solution)/shard_map/while/body/eval_jaxpr/ppermute | solution.py:12
  290.5 7.9 %collective-permute-done = f32[1,256,256]{2,1,0:T(8,128)S(1)} collective-permute-done((f32[1,256,256]{2,1,0:T(8,128)S(1)}, f32[1,256,256]{2,1,0:T(8,128)S(1)}, u32[]{:S(2)}, u32[]{:S(2)}) %collective-permute-start) | collective-permute-done | bytes 262176 | tf_op jit(solution)/shard_map/while/body/eval_jaxpr/ppermute | solution.py:12
  304.1 7.9 %collective-permute-done = f32[1,256,256]{2,1,0:T(8,128)S(1)} collective-permute-done((f32[1,256,256]{2,1,0:T(8,128)S(1)}, f32[1,256,256]{2,1,0:T(8,128)S(1)}, u32[]{:S(2)}, u32[]{:S(2)}) %collective-permute-start) | collective-permute-done | bytes 262176 | tf_op jit(solution)/shard_map/while/body/eval_jaxpr/ppermute | solution.py:12
  317.7 7.9 %collective-permute-done = f32[1,256,256]{2,1,0:T(8,128)S(1)} collective-permute-done((f32[1,256,256]{2,1,0:T(8,128)S(1)}, f32[1,256,256]{2,1,0:T(8,128)S(1)}, u32[]{:S(2)}, u32[]{:S(2)}) %collective-permute-start) | collective-permute-done | bytes 262176 | tf_op jit(solution)/shard_map/while/body/eval_jaxpr/ppermute | solution.py:12
  331.2 7.9 %collective-permute-done = f32[1,256,256]{2,1,0:T(8,128)S(1)} collective-permute-done((f32[1,256,256]{2,1,0:T(8,128)S(1)}, f32[1,256,256]{2,1,0:T(8,128)S(1)}, u32[]{:S(2)}, u32[]{:S(2)}) %collective-permute-start) | collective-permute-done | bytes 262176 | tf_op jit(solution)/shard_map/while/body/eval_jaxpr/ppermute | solution.py:12
  344.8 7.9 %collective-permute-done = f32[1,256,256]{2,1,0:T(8,128)S(1)} collective-permute-done((f32[1,256,256]{2,1,0:T(8,128)S(1)}, f32[1,256,256]{2,1,0:T(8,128)S(1)}, u32[]{:S(2)}, u32[]{:S(2)}) %collective-permute-start) | collective-permute-done | bytes 262176 | tf_op jit(solution)/shard_map/while/body/eval_jaxpr/ppermute | solution.py:12
  358.4 7.9 %collective-permute-done = f32[1,256,256]{2,1,0:T(8,128)S(1)} collective-permute-done((f32[1,256,256]{2,1,0:T(8,128)S(1)}, f32[1,256,256]{2,1,0:T(8,128)S(1)}, u32[]{:S(2)}, u32[]{:S(2)}) %collective-permute-start) | collective-permute-done | bytes 262176 | tf_op jit(solution)/shard_map/while/body/eval_jaxpr/ppermute | solution.py:12
  372.0 7.9 %collective-permute-done = f32[1,256,256]{2,1,0:T(8,128)S(1)} collective-permute-done((f32[1,256,256]{2,1,0:T(8,128)S(1)}, f32[1,256,256]{2,1,0:T(8,128)S(1)}, u32[]{:S(2)}, u32[]{:S(2)}) %collective-permute-start) | collective-permute-done | bytes 262176 | tf_op jit(solution)/shard_map/while/body/eval_jaxpr/ppermute | solution.py:12
  385.5 7.9 %collective-permute-done = f32[1,256,256]{2,1,0:T(8,128)S(1)} collective-permute-done((f32[1,256,256]{2,1,0:T(8,128)S(1)}, f32[1,256,256]{2,1,0:T(8,128)S(1)}, u32[]{:S(2)}, u32[]{:S(2)}) %collective-permute-start) | collective-permute-done | bytes 262176 | tf_op jit(solution)/shard_map/while/body/eval_jaxpr/ppermute | solution.py:12
  399.1 7.9 %collective-permute-done = f32[1,256,256]{2,1,0:T(8,128)S(1)} collective-permute-done((f32[1,256,256]{2,1,0:T(8,128)S(1)}, f32[1,256,256]{2,1,0:T(8,128)S(1)}, u32[]{:S(2)}, u32[]{:S(2)}) %collective-permute-start) | collective-permute-done | bytes 262176 | tf_op jit(solution)/shard_map/while/body/eval_jaxpr/ppermute | solution.py:12
  412.7 7.9 %collective-permute-done = f32[1,256,256]{2,1,0:T(8,128)S(1)} collective-permute-done((f32[1,256,256]{2,1,0:T(8,128)S(1)}, f32[1,256,256]{2,1,0:T(8,128)S(1)}, u32[]{:S(2)}, u32[]{:S(2)}) %collective-permute-start) | collective-permute-done | bytes 262176 | tf_op jit(solution)/shard_map/while/body/eval_jaxpr/ppermute | solution.py:12
  426.2 7.9 %collective-permute-done = f32[1,256,256]{2,1,0:T(8,128)S(1)} collective-permute-done((f32[1,256,256]{2,1,0:T(8,128)S(1)}, f32[1,256,256]{2,1,0:T(8,128)S(1)}, u32[]{:S(2)}, u32[]{:S(2)}) %collective-permute-start) | collective-permute-done | bytes 262176 | tf_op jit(solution)/shard_map/while/body/eval_jaxpr/ppermute | solution.py:12
  439.8 7.9 %collective-permute-done = f32[1,256,256]{2,1,0:T(8,128)S(1)} collective-permute-done((f32[1,256,256]{2,1,0:T(8,128)S(1)}, f32[1,256,256]{2,1,0:T(8,128)S(1)}, u32[]{:S(2)}, u32[]{:S(2)}) %collective-permute-start) | collective-permute-done | bytes 262176 | tf_op jit(solution)/shard_map/while/body/eval_jaxpr/ppermute | solution.py:12
  456.1 11.2 %all-to-all-start.4 = ((bf16[16,2,2048]{2,1,0:T(2,128)(2,1)}), bf16[16,2,2048]{2,1,0:T(2,128)(2,1)S(1)}, u32[]{:S(2)}, u32[]{:S(2)}) async-start(bf16[16,2,2048]{2,1,0:T(2,128)(2,1)} %reshape.369), calls=%async_computation.4 | async-start | bytes 262144 | tf_op jit(solution)/shard_map/all_to_all | solution.py:127
  470.0 9.2 %all-to-all-done.4 = bf16[16,2,2048]{2,1,0:T(2,128)(2,1)S(1)} async-done(((bf16[16,2,2048]{2,1,0:T(2,128)(2,1)}), bf16[16,2,2048]{2,1,0:T(2,128)(2,1)S(1)}, u32[]{:S(2)}, u32[]{:S(2)}) %all-to-all-start.4) | async-done | bytes 131104 | tf_op jit(solution)/shard_map/all_to_all | solution.py:127
  484.6 10.4 %all-to-all-done.2 = bf16[16,2,2048]{2,1,0:T(2,128)(2,1)S(1)} async-done(((bf16[16,2,2048]{2,1,0:T(2,128)(2,1)}), bf16[16,2,2048]{2,1,0:T(2,128)(2,1)S(1)}, u32[]{:S(2)}, u32[]{:S(2)}) %all-to-all-start.2) | async-done | bytes 131104 | tf_op jit(solution)/shard_map/all_to_all | solution.py:126
  498.3 129.8 %psum.7 = f32[]{:T(128)} all-reduce(f32[]{:T(128)S(6)} %add.89), channel_id=1, replica_groups=mesh['seq'=32,'key'=16] {'seq','key'}, use_global_device_ids=true, to_apply=%region_10.11 | all-reduce | flops 1 | bytes 8 | tf_op jit(solution)/shard_map/psum | solution.py:131
  (355 shorter events, 371.1 us)
Async XLA Ops:
  0.7 27.9 %all-to-all-start.1 = ((bf16[256,16,16]{0,2,1:T(8,128)(2,1)}), bf16[256,16,16]{0,2,1:T(8,128)(2,1)S(1)}, u32[]{:S(2)}, u32[]{:S(2)}) async-start(bf16[256,16,16]{0,2,1:T(8,128)(2,1)} %param.15), calls=%async_computation.1 | async-start | bytes 262144 | tf_op jit(solution)/shard_map/all_to_all | solution.py:53
  28.6 17.9 %all-to-all-start.3 = ((bf16[256,16,16]{0,2,1:T(8,128)(2,1)}), bf16[256,16,16]{0,2,1:T(8,128)(2,1)S(1)}, u32[]{:S(2)}, u32[]{:S(2)}) async-start(bf16[256,16,16]{0,2,1:T(8,128)(2,1)} %param.14), calls=%async_computation.3 | async-start | bytes 262144 | tf_op jit(solution)/shard_map/all_to_all | solution.py:52
  46.5 405.4 %all-to-all-start = ((bf16[2,16,16,256]{3,2,0,1:T(8,128)(2,1)}), bf16[2,16,16,256]{3,2,0,1:T(8,128)(2,1)S(1)}, u32[]{:S(2)}, u32[]{:S(2)}) async-start(bf16[2,16,16,256]{3,2,0,1:T(8,128)(2,1)} %copy.117), calls=%async_computation | async-start | bytes 524288 | tf_op jit(solution)/shard_map/all_to_all | solution.py:54
  57.7 9.4 %collective-permute-start = (f32[1,256,256]{2,1,0:T(8,128)S(1)}, f32[1,256,256]{2,1,0:T(8,128)S(1)}, u32[]{:S(2)}, u32[]{:S(2)}) collective-permute-start(f32[1,256,256]{2,1,0:T(8,128)S(1)} %get-tuple-element.637), channel_id=1, source_target_pairs={{16,0},{32,16},{48,32},{64,48},{80,64},{96,80},{112,96},{128,112},... | collective-permute-start | bytes 786440 | tf_op jit(solution)/shard_map/while/body/eval_jaxpr/ppermute | solution.py:12
  71.0 7.7 %collective-permute-start = (f32[1,256,256]{2,1,0:T(8,128)S(1)}, f32[1,256,256]{2,1,0:T(8,128)S(1)}, u32[]{:S(2)}, u32[]{:S(2)}) collective-permute-start(f32[1,256,256]{2,1,0:T(8,128)S(1)} %get-tuple-element.637), channel_id=1, source_target_pairs={{16,0},{32,16},{48,32},{64,48},{80,64},{96,80},{112,96},{128,112},... | collective-permute-start | bytes 786440 | tf_op jit(solution)/shard_map/while/body/eval_jaxpr/ppermute | solution.py:12
  82.4 7.7 %collective-permute-start = (f32[1,256,256]{2,1,0:T(8,128)S(1)}, f32[1,256,256]{2,1,0:T(8,128)S(1)}, u32[]{:S(2)}, u32[]{:S(2)}) collective-permute-start(f32[1,256,256]{2,1,0:T(8,128)S(1)} %get-tuple-element.637), channel_id=1, source_target_pairs={{16,0},{32,16},{48,32},{64,48},{80,64},{96,80},{112,96},{128,112},... | collective-permute-start | bytes 786440 | tf_op jit(solution)/shard_map/while/body/eval_jaxpr/ppermute | solution.py:12
  105.4 7.7 %collective-permute-start = (f32[1,256,256]{2,1,0:T(8,128)S(1)}, f32[1,256,256]{2,1,0:T(8,128)S(1)}, u32[]{:S(2)}, u32[]{:S(2)}) collective-permute-start(f32[1,256,256]{2,1,0:T(8,128)S(1)} %get-tuple-element.637), channel_id=1, source_target_pairs={{16,0},{32,16},{48,32},{64,48},{80,64},{96,80},{112,96},{128,112},... | collective-permute-start | bytes 786440 | tf_op jit(solution)/shard_map/while/body/eval_jaxpr/ppermute | solution.py:12
  116.8 7.7 %collective-permute-start = (f32[1,256,256]{2,1,0:T(8,128)S(1)}, f32[1,256,256]{2,1,0:T(8,128)S(1)}, u32[]{:S(2)}, u32[]{:S(2)}) collective-permute-start(f32[1,256,256]{2,1,0:T(8,128)S(1)} %get-tuple-element.637), channel_id=1, source_target_pairs={{16,0},{32,16},{48,32},{64,48},{80,64},{96,80},{112,96},{128,112},... | collective-permute-start | bytes 786440 | tf_op jit(solution)/shard_map/while/body/eval_jaxpr/ppermute | solution.py:12
  139.7 7.7 %collective-permute-start = (f32[1,256,256]{2,1,0:T(8,128)S(1)}, f32[1,256,256]{2,1,0:T(8,128)S(1)}, u32[]{:S(2)}, u32[]{:S(2)}) collective-permute-start(f32[1,256,256]{2,1,0:T(8,128)S(1)} %get-tuple-element.637), channel_id=1, source_target_pairs={{16,0},{32,16},{48,32},{64,48},{80,64},{96,80},{112,96},{128,112},... | collective-permute-start | bytes 786440 | tf_op jit(solution)/shard_map/while/body/eval_jaxpr/ppermute | solution.py:12
  151.2 7.7 %collective-permute-start = (f32[1,256,256]{2,1,0:T(8,128)S(1)}, f32[1,256,256]{2,1,0:T(8,128)S(1)}, u32[]{:S(2)}, u32[]{:S(2)}) collective-permute-start(f32[1,256,256]{2,1,0:T(8,128)S(1)} %get-tuple-element.637), channel_id=1, source_target_pairs={{16,0},{32,16},{48,32},{64,48},{80,64},{96,80},{112,96},{128,112},... | collective-permute-start | bytes 786440 | tf_op jit(solution)/shard_map/while/body/eval_jaxpr/ppermute | solution.py:12
  174.1 7.7 %collective-permute-start = (f32[1,256,256]{2,1,0:T(8,128)S(1)}, f32[1,256,256]{2,1,0:T(8,128)S(1)}, u32[]{:S(2)}, u32[]{:S(2)}) collective-permute-start(f32[1,256,256]{2,1,0:T(8,128)S(1)} %get-tuple-element.637), channel_id=1, source_target_pairs={{16,0},{32,16},{48,32},{64,48},{80,64},{96,80},{112,96},{128,112},... | collective-permute-start | bytes 786440 | tf_op jit(solution)/shard_map/while/body/eval_jaxpr/ppermute | solution.py:12
  185.6 7.7 %collective-permute-start = (f32[1,256,256]{2,1,0:T(8,128)S(1)}, f32[1,256,256]{2,1,0:T(8,128)S(1)}, u32[]{:S(2)}, u32[]{:S(2)}) collective-permute-start(f32[1,256,256]{2,1,0:T(8,128)S(1)} %get-tuple-element.637), channel_id=1, source_target_pairs={{16,0},{32,16},{48,32},{64,48},{80,64},{96,80},{112,96},{128,112},... | collective-permute-start | bytes 786440 | tf_op jit(solution)/shard_map/while/body/eval_jaxpr/ppermute | solution.py:12
  208.5 8.4 %collective-permute-start = (f32[1,256,256]{2,1,0:T(8,128)S(1)}, f32[1,256,256]{2,1,0:T(8,128)S(1)}, u32[]{:S(2)}, u32[]{:S(2)}) collective-permute-start(f32[1,256,256]{2,1,0:T(8,128)S(1)} %get-tuple-element.637), channel_id=1, source_target_pairs={{16,0},{32,16},{48,32},{64,48},{80,64},{96,80},{112,96},{128,112},... | collective-permute-start | bytes 786440 | tf_op jit(solution)/shard_map/while/body/eval_jaxpr/ppermute | solution.py:12
  220.7 9.8 %collective-permute-start = (f32[1,256,256]{2,1,0:T(8,128)S(1)}, f32[1,256,256]{2,1,0:T(8,128)S(1)}, u32[]{:S(2)}, u32[]{:S(2)}) collective-permute-start(f32[1,256,256]{2,1,0:T(8,128)S(1)} %get-tuple-element.637), channel_id=1, source_target_pairs={{16,0},{32,16},{48,32},{64,48},{80,64},{96,80},{112,96},{128,112},... | collective-permute-start | bytes 786440 | tf_op jit(solution)/shard_map/while/body/eval_jaxpr/ppermute | solution.py:12
  234.3 9.8 %collective-permute-start = (f32[1,256,256]{2,1,0:T(8,128)S(1)}, f32[1,256,256]{2,1,0:T(8,128)S(1)}, u32[]{:S(2)}, u32[]{:S(2)}) collective-permute-start(f32[1,256,256]{2,1,0:T(8,128)S(1)} %get-tuple-element.637), channel_id=1, source_target_pairs={{16,0},{32,16},{48,32},{64,48},{80,64},{96,80},{112,96},{128,112},... | collective-permute-start | bytes 786440 | tf_op jit(solution)/shard_map/while/body/eval_jaxpr/ppermute | solution.py:12
  247.9 9.8 %collective-permute-start = (f32[1,256,256]{2,1,0:T(8,128)S(1)}, f32[1,256,256]{2,1,0:T(8,128)S(1)}, u32[]{:S(2)}, u32[]{:S(2)}) collective-permute-start(f32[1,256,256]{2,1,0:T(8,128)S(1)} %get-tuple-element.637), channel_id=1, source_target_pairs={{16,0},{32,16},{48,32},{64,48},{80,64},{96,80},{112,96},{128,112},... | collective-permute-start | bytes 786440 | tf_op jit(solution)/shard_map/while/body/eval_jaxpr/ppermute | solution.py:12
  261.4 9.8 %collective-permute-start = (f32[1,256,256]{2,1,0:T(8,128)S(1)}, f32[1,256,256]{2,1,0:T(8,128)S(1)}, u32[]{:S(2)}, u32[]{:S(2)}) collective-permute-start(f32[1,256,256]{2,1,0:T(8,128)S(1)} %get-tuple-element.637), channel_id=1, source_target_pairs={{16,0},{32,16},{48,32},{64,48},{80,64},{96,80},{112,96},{128,112},... | collective-permute-start | bytes 786440 | tf_op jit(solution)/shard_map/while/body/eval_jaxpr/ppermute | solution.py:12
  275.0 9.8 %collective-permute-start = (f32[1,256,256]{2,1,0:T(8,128)S(1)}, f32[1,256,256]{2,1,0:T(8,128)S(1)}, u32[]{:S(2)}, u32[]{:S(2)}) collective-permute-start(f32[1,256,256]{2,1,0:T(8,128)S(1)} %get-tuple-element.637), channel_id=1, source_target_pairs={{16,0},{32,16},{48,32},{64,48},{80,64},{96,80},{112,96},{128,112},... | collective-permute-start | bytes 786440 | tf_op jit(solution)/shard_map/while/body/eval_jaxpr/ppermute | solution.py:12
  288.6 9.8 %collective-permute-start = (f32[1,256,256]{2,1,0:T(8,128)S(1)}, f32[1,256,256]{2,1,0:T(8,128)S(1)}, u32[]{:S(2)}, u32[]{:S(2)}) collective-permute-start(f32[1,256,256]{2,1,0:T(8,128)S(1)} %get-tuple-element.637), channel_id=1, source_target_pairs={{16,0},{32,16},{48,32},{64,48},{80,64},{96,80},{112,96},{128,112},... | collective-permute-start | bytes 786440 | tf_op jit(solution)/shard_map/while/body/eval_jaxpr/ppermute | solution.py:12
  302.2 9.8 %collective-permute-start = (f32[1,256,256]{2,1,0:T(8,128)S(1)}, f32[1,256,256]{2,1,0:T(8,128)S(1)}, u32[]{:S(2)}, u32[]{:S(2)}) collective-permute-start(f32[1,256,256]{2,1,0:T(8,128)S(1)} %get-tuple-element.637), channel_id=1, source_target_pairs={{16,0},{32,16},{48,32},{64,48},{80,64},{96,80},{112,96},{128,112},... | collective-permute-start | bytes 786440 | tf_op jit(solution)/shard_map/while/body/eval_jaxpr/ppermute | solution.py:12
  315.7 9.8 %collective-permute-start = (f32[1,256,256]{2,1,0:T(8,128)S(1)}, f32[1,256,256]{2,1,0:T(8,128)S(1)}, u32[]{:S(2)}, u32[]{:S(2)}) collective-permute-start(f32[1,256,256]{2,1,0:T(8,128)S(1)} %get-tuple-element.637), channel_id=1, source_target_pairs={{16,0},{32,16},{48,32},{64,48},{80,64},{96,80},{112,96},{128,112},... | collective-permute-start | bytes 786440 | tf_op jit(solution)/shard_map/while/body/eval_jaxpr/ppermute | solution.py:12
  329.3 9.8 %collective-permute-start = (f32[1,256,256]{2,1,0:T(8,128)S(1)}, f32[1,256,256]{2,1,0:T(8,128)S(1)}, u32[]{:S(2)}, u32[]{:S(2)}) collective-permute-start(f32[1,256,256]{2,1,0:T(8,128)S(1)} %get-tuple-element.637), channel_id=1, source_target_pairs={{16,0},{32,16},{48,32},{64,48},{80,64},{96,80},{112,96},{128,112},... | collective-permute-start | bytes 786440 | tf_op jit(solution)/shard_map/while/body/eval_jaxpr/ppermute | solution.py:12
  342.9 9.8 %collective-permute-start = (f32[1,256,256]{2,1,0:T(8,128)S(1)}, f32[1,256,256]{2,1,0:T(8,128)S(1)}, u32[]{:S(2)}, u32[]{:S(2)}) collective-permute-start(f32[1,256,256]{2,1,0:T(8,128)S(1)} %get-tuple-element.637), channel_id=1, source_target_pairs={{16,0},{32,16},{48,32},{64,48},{80,64},{96,80},{112,96},{128,112},... | collective-permute-start | bytes 786440 | tf_op jit(solution)/shard_map/while/body/eval_jaxpr/ppermute | solution.py:12
  356.5 9.8 %collective-permute-start = (f32[1,256,256]{2,1,0:T(8,128)S(1)}, f32[1,256,256]{2,1,0:T(8,128)S(1)}, u32[]{:S(2)}, u32[]{:S(2)}) collective-permute-start(f32[1,256,256]{2,1,0:T(8,128)S(1)} %get-tuple-element.637), channel_id=1, source_target_pairs={{16,0},{32,16},{48,32},{64,48},{80,64},{96,80},{112,96},{128,112},... | collective-permute-start | bytes 786440 | tf_op jit(solution)/shard_map/while/body/eval_jaxpr/ppermute | solution.py:12
  370.0 9.8 %collective-permute-start = (f32[1,256,256]{2,1,0:T(8,128)S(1)}, f32[1,256,256]{2,1,0:T(8,128)S(1)}, u32[]{:S(2)}, u32[]{:S(2)}) collective-permute-start(f32[1,256,256]{2,1,0:T(8,128)S(1)} %get-tuple-element.637), channel_id=1, source_target_pairs={{16,0},{32,16},{48,32},{64,48},{80,64},{96,80},{112,96},{128,112},... | collective-permute-start | bytes 786440 | tf_op jit(solution)/shard_map/while/body/eval_jaxpr/ppermute | solution.py:12
  383.6 9.8 %collective-permute-start = (f32[1,256,256]{2,1,0:T(8,128)S(1)}, f32[1,256,256]{2,1,0:T(8,128)S(1)}, u32[]{:S(2)}, u32[]{:S(2)}) collective-permute-start(f32[1,256,256]{2,1,0:T(8,128)S(1)} %get-tuple-element.637), channel_id=1, source_target_pairs={{16,0},{32,16},{48,32},{64,48},{80,64},{96,80},{112,96},{128,112},... | collective-permute-start | bytes 786440 | tf_op jit(solution)/shard_map/while/body/eval_jaxpr/ppermute | solution.py:12
  397.2 9.8 %collective-permute-start = (f32[1,256,256]{2,1,0:T(8,128)S(1)}, f32[1,256,256]{2,1,0:T(8,128)S(1)}, u32[]{:S(2)}, u32[]{:S(2)}) collective-permute-start(f32[1,256,256]{2,1,0:T(8,128)S(1)} %get-tuple-element.637), channel_id=1, source_target_pairs={{16,0},{32,16},{48,32},{64,48},{80,64},{96,80},{112,96},{128,112},... | collective-permute-start | bytes 786440 | tf_op jit(solution)/shard_map/while/body/eval_jaxpr/ppermute | solution.py:12
  410.7 9.8 %collective-permute-start = (f32[1,256,256]{2,1,0:T(8,128)S(1)}, f32[1,256,256]{2,1,0:T(8,128)S(1)}, u32[]{:S(2)}, u32[]{:S(2)}) collective-permute-start(f32[1,256,256]{2,1,0:T(8,128)S(1)} %get-tuple-element.637), channel_id=1, source_target_pairs={{16,0},{32,16},{48,32},{64,48},{80,64},{96,80},{112,96},{128,112},... | collective-permute-start | bytes 786440 | tf_op jit(solution)/shard_map/while/body/eval_jaxpr/ppermute | solution.py:12
  424.3 9.8 %collective-permute-start = (f32[1,256,256]{2,1,0:T(8,128)S(1)}, f32[1,256,256]{2,1,0:T(8,128)S(1)}, u32[]{:S(2)}, u32[]{:S(2)}) collective-permute-start(f32[1,256,256]{2,1,0:T(8,128)S(1)} %get-tuple-element.637), channel_id=1, source_target_pairs={{16,0},{32,16},{48,32},{64,48},{80,64},{96,80},{112,96},{128,112},... | collective-permute-start | bytes 786440 | tf_op jit(solution)/shard_map/while/body/eval_jaxpr/ppermute | solution.py:12
  437.9 9.8 %collective-permute-start = (f32[1,256,256]{2,1,0:T(8,128)S(1)}, f32[1,256,256]{2,1,0:T(8,128)S(1)}, u32[]{:S(2)}, u32[]{:S(2)}) collective-permute-start(f32[1,256,256]{2,1,0:T(8,128)S(1)} %get-tuple-element.637), channel_id=1, source_target_pairs={{16,0},{32,16},{48,32},{64,48},{80,64},{96,80},{112,96},{128,112},... | collective-permute-start | bytes 786440 | tf_op jit(solution)/shard_map/while/body/eval_jaxpr/ppermute | solution.py:12
  456.1 23.1 %all-to-all-start.4 = ((bf16[16,2,2048]{2,1,0:T(2,128)(2,1)}), bf16[16,2,2048]{2,1,0:T(2,128)(2,1)S(1)}, u32[]{:S(2)}, u32[]{:S(2)}) async-start(bf16[16,2,2048]{2,1,0:T(2,128)(2,1)} %reshape.369), calls=%async_computation.4 | async-start | bytes 262144 | tf_op jit(solution)/shard_map/all_to_all | solution.py:127
  479.2 15.8 %all-to-all-start.2 = ((bf16[16,2,2048]{2,1,0:T(2,128)(2,1)}), bf16[16,2,2048]{2,1,0:T(2,128)(2,1)S(1)}, u32[]{:S(2)}, u32[]{:S(2)}) async-start(bf16[16,2,2048]{2,1,0:T(2,128)(2,1)} %reshape.367), calls=%async_computation.2 | async-start | bytes 262144 | tf_op jit(solution)/shard_map/all_to_all | solution.py:126
  (10 other events, 119.9 us)
where the time goes:
time: 636 us; the launch traced here: 631 us
  waiting for transfers between devices  255 us (40%)
  blocking collectives  130 us (20%)
  starting transfers between devices  104 us (16%)
  matrix products  84.9 us (13%)
  local copies, waits for them, and re-layouts  45.3 us (7%)
    ppermute x31, waiting for transfers between devices, from_behind(): lax.ppermute(value, axis, [(source, source + steps) for source in range(f...  215 us
    psum x1, blocking collectives, local(): summed = lax.psum(partial_value, ('seq', 'key'))  130 us
    dot_general x130, matrix products, precise_product(): jnp.einsum(form, left.astype(jnp.float32), right, precision=highest_mode)  80.6 us
    ppermute x31, starting transfers between devices, from_behind(): lax.ppermute(value, axis, [(source, source + steps) for source in range(f...  61.5 us
    dynamic_slice x64, local copies, waits for them, and re-layouts, device_map(): lax.scan(group_step, state_out, (written_keys, key_result, end_decay, off...  37.6 us
    all_to_all x1, starting transfers between devices, local(): lax.all_to_all(key_rows, 'key', split_axis=1, concat_axis=2, tiled=True)  15.9 us
  transfers between devices with their start and end apart: 36, of which 35 were waited for; matrix products, arithmetic and copies ran while one was open for 20% of the time, Pallas kernels for 0%

commit v1 on v0

--- a/solution.py
+++ b/solution.py
@@ -128,7 +128,7 @@
     )
     value_square = square_sum(grad_value)
     partial_value = square_sum(grad_query) + square_sum(grad_key) + value_square
-    summed = lax.psum(partial_value, ("seq", "key"))
+    summed = lax.psum(lax.psum(partial_value, "seq"), "key")
     entries = (
         token_count * lax.axis_size("seq") * query_rows.shape[1] * (2 * key_width + value_width)
     )

time: 636 us -> 618 us (0.972)
  the two profiles are of different devices: /device:TPU:1 before, /device:TPU:6 now
where the time goes in v1:
time: 618 us; the launch traced here: 614 us
  starting transfers between devices  220 us (36%)
  waiting for transfers between devices  167 us (27%)
  matrix products  84.9 us (14%)
  blocking collectives  84.1 us (14%)
  local copies, waits for them, and re-layouts  45.3 us (7%)
    ppermute x31, starting transfers between devices, from_behind(): lax.ppermute(value, axis, [(source, source + steps) for source in range(f...  181 us
    ppermute x31, waiting for transfers between devices, from_behind(): lax.ppermute(value, axis, [(source, source + steps) for source in range(f...  120 us
    psum x2, blocking collectives, local(): summed = lax.psum(lax.psum(partial_value, 'seq'), 'key')  84.1 us
    dot_general x130, matrix products, precise_product(): jnp.einsum(form, left.astype(jnp.float32), right, precision=highest_mode)  80.6 us
    dynamic_slice x64, local copies, waits for them, and re-layouts, device_map(): lax.scan(group_step, state_out, (written_keys, key_result, end_decay, off...  37.6 us
    all_to_all x1, starting transfers between devices, local(): lax.all_to_all(key_rows, 'key', split_axis=1, concat_axis=2, tiled=True)  15.3 us
    all_to_all x1, waiting for transfers between devices, local(): lax.all_to_all(key_rows, 'key', split_axis=1, concat_axis=2, tiled=True)  13.4 us
  transfers between devices with their start and end apart: 36, of which 35 were waited for; matrix products, arithmetic and copies ran while one was open for 21% of the time, Pallas kernels for 0%

profile of v1, /device:TPU:6, one launch (start us, length us, event | category | flops | bytes accessed | tf_op | source)
XLA Modules:
  0.0 613.5 jit_solution(12314873346037655857)
XLA Ops:
  0.7 15.3 %all-to-all-start.1 = ((bf16[256,16,16]{0,2,1:T(8,128)(2,1)}), bf16[256,16,16]{0,2,1:T(8,128)(2,1)S(1)}, u32[]{:S(2)}, u32[]{:S(2)}) async-start(bf16[256,16,16]{0,2,1:T(8,128)(2,1)} %param.15), calls=%async_computation.1 | async-start | bytes 262144 | tf_op jit(solution)/shard_map/all_to_all | solution.py:53
  17.3 13.4 %all-to-all-done.1 = bf16[256,16,16]{0,2,1:T(8,128)(2,1)S(1)} async-done(((bf16[256,16,16]{0,2,1:T(8,128)(2,1)}), bf16[256,16,16]{0,2,1:T(8,128)(2,1)S(1)}, u32[]{:S(2)}, u32[]{:S(2)}) %all-to-all-start.1) | async-done | bytes 131104 | tf_op jit(solution)/shard_map/all_to_all | solution.py:53
  36.9 11.7 %all-to-all-done.3 = bf16[256,16,16]{0,2,1:T(8,128)(2,1)S(1)} async-done(((bf16[256,16,16]{0,2,1:T(8,128)(2,1)}), bf16[256,16,16]{0,2,1:T(8,128)(2,1)S(1)}, u32[]{:S(2)}, u32[]{:S(2)}) %all-to-all-start.3) | async-done | bytes 131104 | tf_op jit(solution)/shard_map/all_to_all | solution.py:52
  54.5 418.4 %while.57 = (s32[]{:T(128)}, f32[1,256,256]{2,1,0:T(8,128)S(1)}, f32[2,1]{0,1:T(1,128)S(1)}, bf16[2,128,1,256]{3,1,2,0:T(8,128)(2,1)S(1)}, bf16[2,128,1,256]{3,1...) while((s32[]{:T(128)}, f32[1,256,256]{2,1,0:T(8,128)S(1)}, ...), condition=%wide.region_4.5_spmd, body=%wide.region_1.4_spmd.sunk | while | flops 201523200 | bytes 3015986 | solution.py:97
  69.2 6.2 %collective-permute-start = (f32[1,256,256]{2,1,0:T(8,128)S(1)}, f32[1,256,256]{2,1,0:T(8,128)S(1)}, u32[]{:S(2)}, u32[]{:S(2)}) collective-permute-start(f32[1,256,256]{2,1,0:T(8,128)S(1)} %get-tuple-element.637), channel_id=1, source_target_pairs={{16,0},{32,16},{48,32},{64,48},{80,64},{96,80},{112,96},{128,112},... | collective-permute-start | bytes 786440 | tf_op jit(solution)/shard_map/while/body/eval_jaxpr/ppermute | solution.py:12
  83.1 5.9 collective-permute-start
  96.6 5.9 collective-permute-start
  110.2 5.9 collective-permute-start
  123.8 5.9 collective-permute-start
  137.3 5.9 collective-permute-start
  164.5 5.9 collective-permute-start
  178.1 5.9 collective-permute-start
  191.6 5.9 collective-permute-start
  218.8 5.9 collective-permute-start
  232.4 5.9 collective-permute-start
  259.5 5.9 collective-permute-start
  273.1 5.9 collective-permute-start
  286.7 5.9 collective-permute-start
  313.8 5.9 collective-permute-start
  327.4 5.9 collective-permute-start
  354.5 5.9 collective-permute-start
  368.1 5.9 collective-permute-start
  381.7 5.9 collective-permute-start
  408.8 5.9 collective-permute-start
  422.4 5.9 collective-permute-start
  449.5 5.9 collective-permute-start
  463.1 5.9 collective-permute-start
  481.3 11.4 %all-to-all-start.4 = ((bf16[16,2,2048]{2,1,0:T(2,128)(2,1)}), bf16[16,2,2048]{2,1,0:T(2,128)(2,1)S(1)}, u32[]{:S(2)}, u32[]{:S(2)}) async-start(bf16[16,2,2048]{2,1,0:T(2,128)(2,1)} %reshape.369), calls=%async_computation.4 | async-start | bytes 262144 | tf_op jit(solution)/shard_map/all_to_all | solution.py:127
  495.5 10.5 %all-to-all-done.4 = bf16[16,2,2048]{2,1,0:T(2,128)(2,1)S(1)} async-done(((bf16[16,2,2048]{2,1,0:T(2,128)(2,1)}), bf16[16,2,2048]{2,1,0:T(2,128)(2,1)S(1)}, u32[]{:S(2)}, u32[]{:S(2)}) %all-to-all-start.4) | async-done | bytes 131104 | tf_op jit(solution)/shard_map/all_to_all | solution.py:127
  511.5 11.6 %all-to-all-done.2 = bf16[16,2,2048]{2,1,0:T(2,128)(2,1)S(1)} async-done(((bf16[16,2,2048]{2,1,0:T(2,128)(2,1)}), bf16[16,2,2048]{2,1,0:T(2,128)(2,1)S(1)}, u32[]{:S(2)}, u32[]{:S(2)}) %all-to-all-start.2) | async-done | bytes 131104 | tf_op jit(solution)/shard_map/all_to_all | solution.py:126
  526.3 54.7 %psum.14 = f32[]{:T(128)} all-reduce(f32[]{:T(128)S(6)} %add.91), channel_id=1, replica_groups=mesh['seq'=32,'key'=16] {'seq'}, use_global_device_ids=true, to_apply=%region_10.11 | all-reduce | flops 1 | bytes 8 | tf_op jit(solution)/shard_map/psum | solution.py:131
  581.0 29.4 %psum.15 = f32[]{:T(128)} all-reduce(f32[]{:T(128)} %psum.14), channel_id=1, replica_groups=mesh['seq'=32,'key'=16] {'key'}, use_global_device_ids=true, to_apply=%region_11.12 | all-reduce | flops 1 | bytes 8 | tf_op jit(solution)/shard_map/psum | solution.py:131
  (356 shorter events, 430.7 us)
Async XLA Ops:
  0.7 30.0 %all-to-all-start.1 = ((bf16[256,16,16]{0,2,1:T(8,128)(2,1)}), bf16[256,16,16]{0,2,1:T(8,128)(2,1)S(1)}, u32[]{:S(2)}, u32[]{:S(2)}) async-start(bf16[256,16,16]{0,2,1:T(8,128)(2,1)} %param.15), calls=%async_computation.1 | async-start | bytes 262144 | tf_op jit(solution)/shard_map/all_to_all | solution.py:53
  30.7 17.9 %all-to-all-start.3 = ((bf16[256,16,16]{0,2,1:T(8,128)(2,1)}), bf16[256,16,16]{0,2,1:T(8,128)(2,1)S(1)}, u32[]{:S(2)}, u32[]{:S(2)}) async-start(bf16[256,16,16]{0,2,1:T(8,128)(2,1)} %param.14), calls=%async_computation.3 | async-start | bytes 262144 | tf_op jit(solution)/shard_map/all_to_all | solution.py:52
  48.6 428.6 %all-to-all-start = ((bf16[2,16,16,256]{3,2,0,1:T(8,128)(2,1)}), bf16[2,16,16,256]{3,2,0,1:T(8,128)(2,1)S(1)}, u32[]{:S(2)}, u32[]{:S(2)}) async-start(bf16[2,16,16,256]{3,2,0,1:T(8,128)(2,1)} %copy.117), calls=%async_computation | async-start | bytes 524288 | tf_op jit(solution)/shard_map/all_to_all | solution.py:54
  69.2 10.1 %collective-permute-start = (f32[1,256,256]{2,1,0:T(8,128)S(1)}, f32[1,256,256]{2,1,0:T(8,128)S(1)}, u32[]{:S(2)}, u32[]{:S(2)}) collective-permute-start(f32[1,256,256]{2,1,0:T(8,128)S(1)} %get-tuple-element.637), channel_id=1, source_target_pairs={{16,0},{32,16},{48,32},{64,48},{80,64},{96,80},{112,96},{128,112},... | collective-permute-start | bytes 786440 | tf_op jit(solution)/shard_map/while/body/eval_jaxpr/ppermute | solution.py:12
  83.1 9.8 %collective-permute-start = (f32[1,256,256]{2,1,0:T(8,128)S(1)}, f32[1,256,256]{2,1,0:T(8,128)S(1)}, u32[]{:S(2)}, u32[]{:S(2)}) collective-permute-start(f32[1,256,256]{2,1,0:T(8,128)S(1)} %get-tuple-element.637), channel_id=1, source_target_pairs={{16,0},{32,16},{48,32},{64,48},{80,64},{96,80},{112,96},{128,112},... | collective-permute-start | bytes 786440 | tf_op jit(solution)/shard_map/while/body/eval_jaxpr/ppermute | solution.py:12
  96.6 9.8 %collective-permute-start = (f32[1,256,256]{2,1,0:T(8,128)S(1)}, f32[1,256,256]{2,1,0:T(8,128)S(1)}, u32[]{:S(2)}, u32[]{:S(2)}) collective-permute-start(f32[1,256,256]{2,1,0:T(8,128)S(1)} %get-tuple-element.637), channel_id=1, source_target_pairs={{16,0},{32,16},{48,32},{64,48},{80,64},{96,80},{112,96},{128,112},... | collective-permute-start | bytes 786440 | tf_op jit(solution)/shard_map/while/body/eval_jaxpr/ppermute | solution.py:12
  110.2 9.8 %collective-permute-start = (f32[1,256,256]{2,1,0:T(8,128)S(1)}, f32[1,256,256]{2,1,0:T(8,128)S(1)}, u32[]{:S(2)}, u32[]{:S(2)}) collective-permute-start(f32[1,256,256]{2,1,0:T(8,128)S(1)} %get-tuple-element.637), channel_id=1, source_target_pairs={{16,0},{32,16},{48,32},{64,48},{80,64},{96,80},{112,96},{128,112},... | collective-permute-start | bytes 786440 | tf_op jit(solution)/shard_map/while/body/eval_jaxpr/ppermute | solution.py:12
  123.8 9.8 %collective-permute-start = (f32[1,256,256]{2,1,0:T(8,128)S(1)}, f32[1,256,256]{2,1,0:T(8,128)S(1)}, u32[]{:S(2)}, u32[]{:S(2)}) collective-permute-start(f32[1,256,256]{2,1,0:T(8,128)S(1)} %get-tuple-element.637), channel_id=1, source_target_pairs={{16,0},{32,16},{48,32},{64,48},{80,64},{96,80},{112,96},{128,112},... | collective-permute-start | bytes 786440 | tf_op jit(solution)/shard_map/while/body/eval_jaxpr/ppermute | solution.py:12
  137.3 9.8 %collective-permute-start = (f32[1,256,256]{2,1,0:T(8,128)S(1)}, f32[1,256,256]{2,1,0:T(8,128)S(1)}, u32[]{:S(2)}, u32[]{:S(2)}) collective-permute-start(f32[1,256,256]{2,1,0:T(8,128)S(1)} %get-tuple-element.637), channel_id=1, source_target_pairs={{16,0},{32,16},{48,32},{64,48},{80,64},{96,80},{112,96},{128,112},... | collective-permute-start | bytes 786440 | tf_op jit(solution)/shard_map/while/body/eval_jaxpr/ppermute | solution.py:12
  150.9 9.8 %collective-permute-start = (f32[1,256,256]{2,1,0:T(8,128)S(1)}, f32[1,256,256]{2,1,0:T(8,128)S(1)}, u32[]{:S(2)}, u32[]{:S(2)}) collective-permute-start(f32[1,256,256]{2,1,0:T(8,128)S(1)} %get-tuple-element.637), channel_id=1, source_target_pairs={{16,0},{32,16},{48,32},{64,48},{80,64},{96,80},{112,96},{128,112},... | collective-permute-start | bytes 786440 | tf_op jit(solution)/shard_map/while/body/eval_jaxpr/ppermute | solution.py:12
  164.5 9.8 %collective-permute-start = (f32[1,256,256]{2,1,0:T(8,128)S(1)}, f32[1,256,256]{2,1,0:T(8,128)S(1)}, u32[]{:S(2)}, u32[]{:S(2)}) collective-permute-start(f32[1,256,256]{2,1,0:T(8,128)S(1)} %get-tuple-element.637), channel_id=1, source_target_pairs={{16,0},{32,16},{48,32},{64,48},{80,64},{96,80},{112,96},{128,112},... | collective-permute-start | bytes 786440 | tf_op jit(solution)/shard_map/while/body/eval_jaxpr/ppermute | solution.py:12
  178.1 9.8 %collective-permute-start = (f32[1,256,256]{2,1,0:T(8,128)S(1)}, f32[1,256,256]{2,1,0:T(8,128)S(1)}, u32[]{:S(2)}, u32[]{:S(2)}) collective-permute-start(f32[1,256,256]{2,1,0:T(8,128)S(1)} %get-tuple-element.637), channel_id=1, source_target_pairs={{16,0},{32,16},{48,32},{64,48},{80,64},{96,80},{112,96},{128,112},... | collective-permute-start | bytes 786440 | tf_op jit(solution)/shard_map/while/body/eval_jaxpr/ppermute | solution.py:12
  191.6 9.8 %collective-permute-start = (f32[1,256,256]{2,1,0:T(8,128)S(1)}, f32[1,256,256]{2,1,0:T(8,128)S(1)}, u32[]{:S(2)}, u32[]{:S(2)}) collective-permute-start(f32[1,256,256]{2,1,0:T(8,128)S(1)} %get-tuple-element.637), channel_id=1, source_target_pairs={{16,0},{32,16},{48,32},{64,48},{80,64},{96,80},{112,96},{128,112},... | collective-permute-start | bytes 786440 | tf_op jit(solution)/shard_map/while/body/eval_jaxpr/ppermute | solution.py:12
  205.2 9.8 %collective-permute-start = (f32[1,256,256]{2,1,0:T(8,128)S(1)}, f32[1,256,256]{2,1,0:T(8,128)S(1)}, u32[]{:S(2)}, u32[]{:S(2)}) collective-permute-start(f32[1,256,256]{2,1,0:T(8,128)S(1)} %get-tuple-element.637), channel_id=1, source_target_pairs={{16,0},{32,16},{48,32},{64,48},{80,64},{96,80},{112,96},{128,112},... | collective-permute-start | bytes 786440 | tf_op jit(solution)/shard_map/while/body/eval_jaxpr/ppermute | solution.py:12
  218.8 9.8 %collective-permute-start = (f32[1,256,256]{2,1,0:T(8,128)S(1)}, f32[1,256,256]{2,1,0:T(8,128)S(1)}, u32[]{:S(2)}, u32[]{:S(2)}) collective-permute-start(f32[1,256,256]{2,1,0:T(8,128)S(1)} %get-tuple-element.637), channel_id=1, source_target_pairs={{16,0},{32,16},{48,32},{64,48},{80,64},{96,80},{112,96},{128,112},... | collective-permute-start | bytes 786440 | tf_op jit(solution)/shard_map/while/body/eval_jaxpr/ppermute | solution.py:12
  232.4 9.8 %collective-permute-start = (f32[1,256,256]{2,1,0:T(8,128)S(1)}, f32[1,256,256]{2,1,0:T(8,128)S(1)}, u32[]{:S(2)}, u32[]{:S(2)}) collective-permute-start(f32[1,256,256]{2,1,0:T(8,128)S(1)} %get-tuple-element.637), channel_id=1, source_target_pairs={{16,0},{32,16},{48,32},{64,48},{80,64},{96,80},{112,96},{128,112},... | collective-permute-start | bytes 786440 | tf_op jit(solution)/shard_map/while/body/eval_jaxpr/ppermute | solution.py:12
  245.9 9.8 %collective-permute-start = (f32[1,256,256]{2,1,0:T(8,128)S(1)}, f32[1,256,256]{2,1,0:T(8,128)S(1)}, u32[]{:S(2)}, u32[]{:S(2)}) collective-permute-start(f32[1,256,256]{2,1,0:T(8,128)S(1)} %get-tuple-element.637), channel_id=1, source_target_pairs={{16,0},{32,16},{48,32},{64,48},{80,64},{96,80},{112,96},{128,112},... | collective-permute-start | bytes 786440 | tf_op jit(solution)/shard_map/while/body/eval_jaxpr/ppermute | solution.py:12
  259.5 9.8 %collective-permute-start = (f32[1,256,256]{2,1,0:T(8,128)S(1)}, f32[1,256,256]{2,1,0:T(8,128)S(1)}, u32[]{:S(2)}, u32[]{:S(2)}) collective-permute-start(f32[1,256,256]{2,1,0:T(8,128)S(1)} %get-tuple-element.637), channel_id=1, source_target_pairs={{16,0},{32,16},{48,32},{64,48},{80,64},{96,80},{112,96},{128,112},... | collective-permute-start | bytes 786440 | tf_op jit(solution)/shard_map/while/body/eval_jaxpr/ppermute | solution.py:12
  273.1 9.8 %collective-permute-start = (f32[1,256,256]{2,1,0:T(8,128)S(1)}, f32[1,256,256]{2,1,0:T(8,128)S(1)}, u32[]{:S(2)}, u32[]{:S(2)}) collective-permute-start(f32[1,256,256]{2,1,0:T(8,128)S(1)} %get-tuple-element.637), channel_id=1, source_target_pairs={{16,0},{32,16},{48,32},{64,48},{80,64},{96,80},{112,96},{128,112},... | collective-permute-start | bytes 786440 | tf_op jit(solution)/shard_map/while/body/eval_jaxpr/ppermute | solution.py:12
  286.7 9.8 %collective-permute-start = (f32[1,256,256]{2,1,0:T(8,128)S(1)}, f32[1,256,256]{2,1,0:T(8,128)S(1)}, u32[]{:S(2)}, u32[]{:S(2)}) collective-permute-start(f32[1,256,256]{2,1,0:T(8,128)S(1)} %get-tuple-element.637), channel_id=1, source_target_pairs={{16,0},{32,16},{48,32},{64,48},{80,64},{96,80},{112,96},{128,112},... | collective-permute-start | bytes 786440 | tf_op jit(solution)/shard_map/while/body/eval_jaxpr/ppermute | solution.py:12
  300.2 9.8 %collective-permute-start = (f32[1,256,256]{2,1,0:T(8,128)S(1)}, f32[1,256,256]{2,1,0:T(8,128)S(1)}, u32[]{:S(2)}, u32[]{:S(2)}) collective-permute-start(f32[1,256,256]{2,1,0:T(8,128)S(1)} %get-tuple-element.637), channel_id=1, source_target_pairs={{16,0},{32,16},{48,32},{64,48},{80,64},{96,80},{112,96},{128,112},... | collective-permute-start | bytes 786440 | tf_op jit(solution)/shard_map/while/body/eval_jaxpr/ppermute | solution.py:12
  313.8 9.8 %collective-permute-start = (f32[1,256,256]{2,1,0:T(8,128)S(1)}, f32[1,256,256]{2,1,0:T(8,128)S(1)}, u32[]{:S(2)}, u32[]{:S(2)}) collective-permute-start(f32[1,256,256]{2,1,0:T(8,128)S(1)} %get-tuple-element.637), channel_id=1, source_target_pairs={{16,0},{32,16},{48,32},{64,48},{80,64},{96,80},{112,96},{128,112},... | collective-permute-start | bytes 786440 | tf_op jit(solution)/shard_map/while/body/eval_jaxpr/ppermute | solution.py:12
  327.4 9.8 %collective-permute-start = (f32[1,256,256]{2,1,0:T(8,128)S(1)}, f32[1,256,256]{2,1,0:T(8,128)S(1)}, u32[]{:S(2)}, u32[]{:S(2)}) collective-permute-start(f32[1,256,256]{2,1,0:T(8,128)S(1)} %get-tuple-element.637), channel_id=1, source_target_pairs={{16,0},{32,16},{48,32},{64,48},{80,64},{96,80},{112,96},{128,112},... | collective-permute-start | bytes 786440 | tf_op jit(solution)/shard_map/while/body/eval_jaxpr/ppermute | solution.py:12
  354.5 9.8 %collective-permute-start = (f32[1,256,256]{2,1,0:T(8,128)S(1)}, f32[1,256,256]{2,1,0:T(8,128)S(1)}, u32[]{:S(2)}, u32[]{:S(2)}) collective-permute-start(f32[1,256,256]{2,1,0:T(8,128)S(1)} %get-tuple-element.637), channel_id=1, source_target_pairs={{16,0},{32,16},{48,32},{64,48},{80,64},{96,80},{112,96},{128,112},... | collective-permute-start | bytes 786440 | tf_op jit(solution)/shard_map/while/body/eval_jaxpr/ppermute | solution.py:12
  368.1 9.8 %collective-permute-start = (f32[1,256,256]{2,1,0:T(8,128)S(1)}, f32[1,256,256]{2,1,0:T(8,128)S(1)}, u32[]{:S(2)}, u32[]{:S(2)}) collective-permute-start(f32[1,256,256]{2,1,0:T(8,128)S(1)} %get-tuple-element.637), channel_id=1, source_target_pairs={{16,0},{32,16},{48,32},{64,48},{80,64},{96,80},{112,96},{128,112},... | collective-permute-start | bytes 786440 | tf_op jit(solution)/shard_map/while/body/eval_jaxpr/ppermute | solution.py:12
  381.7 9.8 %collective-permute-start = (f32[1,256,256]{2,1,0:T(8,128)S(1)}, f32[1,256,256]{2,1,0:T(8,128)S(1)}, u32[]{:S(2)}, u32[]{:S(2)}) collective-permute-start(f32[1,256,256]{2,1,0:T(8,128)S(1)} %get-tuple-element.637), channel_id=1, source_target_pairs={{16,0},{32,16},{48,32},{64,48},{80,64},{96,80},{112,96},{128,112},... | collective-permute-start | bytes 786440 | tf_op jit(solution)/shard_map/while/body/eval_jaxpr/ppermute | solution.py:12
  408.8 9.8 %collective-permute-start = (f32[1,256,256]{2,1,0:T(8,128)S(1)}, f32[1,256,256]{2,1,0:T(8,128)S(1)}, u32[]{:S(2)}, u32[]{:S(2)}) collective-permute-start(f32[1,256,256]{2,1,0:T(8,128)S(1)} %get-tuple-element.637), channel_id=1, source_target_pairs={{16,0},{32,16},{48,32},{64,48},{80,64},{96,80},{112,96},{128,112},... | collective-permute-start | bytes 786440 | tf_op jit(solution)/shard_map/while/body/eval_jaxpr/ppermute | solution.py:12
  422.4 9.8 %collective-permute-start = (f32[1,256,256]{2,1,0:T(8,128)S(1)}, f32[1,256,256]{2,1,0:T(8,128)S(1)}, u32[]{:S(2)}, u32[]{:S(2)}) collective-permute-start(f32[1,256,256]{2,1,0:T(8,128)S(1)} %get-tuple-element.637), channel_id=1, source_target_pairs={{16,0},{32,16},{48,32},{64,48},{80,64},{96,80},{112,96},{128,112},... | collective-permute-start | bytes 786440 | tf_op jit(solution)/shard_map/while/body/eval_jaxpr/ppermute | solution.py:12
  449.5 9.8 %collective-permute-start = (f32[1,256,256]{2,1,0:T(8,128)S(1)}, f32[1,256,256]{2,1,0:T(8,128)S(1)}, u32[]{:S(2)}, u32[]{:S(2)}) collective-permute-start(f32[1,256,256]{2,1,0:T(8,128)S(1)} %get-tuple-element.637), channel_id=1, source_target_pairs={{16,0},{32,16},{48,32},{64,48},{80,64},{96,80},{112,96},{128,112},... | collective-permute-start | bytes 786440 | tf_op jit(solution)/shard_map/while/body/eval_jaxpr/ppermute | solution.py:12
  463.1 9.8 %collective-permute-start = (f32[1,256,256]{2,1,0:T(8,128)S(1)}, f32[1,256,256]{2,1,0:T(8,128)S(1)}, u32[]{:S(2)}, u32[]{:S(2)}) collective-permute-start(f32[1,256,256]{2,1,0:T(8,128)S(1)} %get-tuple-element.637), channel_id=1, source_target_pairs={{16,0},{32,16},{48,32},{64,48},{80,64},{96,80},{112,96},{128,112},... | collective-permute-start | bytes 786440 | tf_op jit(solution)/shard_map/while/body/eval_jaxpr/ppermute | solution.py:12
  481.3 24.7 %all-to-all-start.4 = ((bf16[16,2,2048]{2,1,0:T(2,128)(2,1)}), bf16[16,2,2048]{2,1,0:T(2,128)(2,1)S(1)}, u32[]{:S(2)}, u32[]{:S(2)}) async-start(bf16[16,2,2048]{2,1,0:T(2,128)(2,1)} %reshape.369), calls=%async_computation.4 | async-start | bytes 262144 | tf_op jit(solution)/shard_map/all_to_all | solution.py:127
  506.0 17.0 %all-to-all-start.2 = ((bf16[16,2,2048]{2,1,0:T(2,128)(2,1)}), bf16[16,2,2048]{2,1,0:T(2,128)(2,1)S(1)}, u32[]{:S(2)}, u32[]{:S(2)}) async-start(bf16[16,2,2048]{2,1,0:T(2,128)(2,1)} %reshape.367), calls=%async_computation.2 | async-start | bytes 262144 | tf_op jit(solution)/shard_map/all_to_all | solution.py:126
  (10 other events, 126.2 us)
